TPU v7x, 32 devices: a whole 2x2x4 slice. The times are simulated.
32 devices in a mesh: batch: 4 (over z), space: 8 (over y, x, core).
Axes of the slice: x: 2, y: 2, z: 4, core: 2. Of those that a mesh axis runs over, the one named last changes fastest.
Arguments:
- density: bfloat16 [8, 4, 16, 16, 256], P('batch', None, 'space'), may hold values from -6 to 6
- w_first: bfloat16 [32, 108], replicated, may hold values from -0.625 to 0.625
- b_first: float32 [32], replicated, may hold values from -3 to 3
- w_second: bfloat16 [64, 864], replicated, may hold values from -0.4375 to 0.4375
- b_second: float32 [64], replicated, may hold values from -3 to 3
- cotangent: bfloat16 [8, 64, 8, 8, 128], P('batch', None, 'space'), may hold values from -6 to 6
Outputs:
- features: bfloat16 [8, 64, 8, 8, 128], P('batch', None, 'space')
- grad_w_first: float32 [32, 108], replicated
- grad_b_first: float32 [32], replicated
- grad_w_second: float32 [64, 864], replicated
- grad_b_second: float32 [64], replicated
All inputs are finite; a program needn't handle non-finite values.
Results may differ from a plain program's by a relative error of at most 0.0095.
Values may be sent and summed in bfloat16 or wider, within the bound.
A program may use at most 128 MiB of HBM per device.

v0:
```python
import functools

import jax
import jax.numpy as jnp
import numpy as np
from jax import lax
from jax.experimental import pallas as pl
from jax.experimental.pallas import tpu as pltpu
from jax.sharding import PartitionSpec as P

F32 = jnp.float32
BF16 = jnp.bfloat16
MESH = pl.DeviceIdType.MESH
NT = (((1,), (1,)), ((), ()))


def fold_matrix():
    fold = np.zeros((128, 8, 256), np.float32)

    def coordinate(group, parity):
        return 1 + parity if group == 0 else (0 if parity == 1 else 3)

    planes = (1, 2, 0, 3)
    for row in range(256):
        zi, xg, yg = row >> 6, (row >> 5) & 1, (row >> 4) & 1
        yp, xp, c = (row >> 3) & 1, (row >> 2) & 1, row & 3
        zz, xx, yy = planes[zi], coordinate(xg, xp), coordinate(yg, yp)
        for pos in range(8):
            i, j, k = zz - (pos >> 2), xx - ((pos >> 1) & 1), yy - (pos & 1)
            if 0 <= i < 3 and 0 <= j < 3 and 0 <= k < 3:
                fold[((i * 3 + j) * 3 + k) * 4 + c, pos, row] = 1
    return fold.reshape(128, 2048)


def iota(shape, axis):
    return lax.broadcasted_iota(jnp.int32, shape, axis)


def sigmoid(value):
    return 0.5 + 0.5 * jnp.tanh(0.5 * value)


def column_of(row):
    size = row.shape[1]
    eye = iota((size, size), 0) == iota((size, size), 1)
    return jnp.sum(jnp.where(eye, row, 0.0), axis=1, keepdims=True)


def row_of(column):
    size = column.shape[0]
    eye = iota((size, size), 0) == iota((size, size), 1)
    return jnp.sum(jnp.where(eye, column, 0.0), axis=0, keepdims=True)


def dot(a, b):
    return jnp.dot(a, b, preferred_element_type=F32)


def dot_nt(a, b):
    return lax.dot_general(a, b, NT, preferred_element_type=F32)


def before(tile):
    axis = tile.ndim - 1
    return jnp.where(iota(tile.shape, axis) == 0, 0.0, pltpu.roll(tile, 1, axis))


def after(tile):
    axis = tile.ndim - 1
    return jnp.where(iota(tile.shape, axis) == 127, 0.0, pltpu.roll(tile, 127, axis))


def kernel(
    nb, ns,
    dens, w1_hbm, b1_hbm, w2_hbm, b2_hbm, cot_hbm, fold_hbm,
    feat, gw1_out, gb1_out, gw2_out, gb2_out,
    w1, b1, w2, b2, cot, fold, buf, cols1, wbig, d1, w1s, w2s, w2c, wb, pooled, halo2, c9, acc2, trans, gs, cb, bsend, brecv, bown, gf,
    part, rs_recv, mine, bx_recv, full, small, sm_recv, sm_mid, sm_recv2,
    load_sem, in_sem, dsend, drecv, psend, precv, ksend, krecv, rsend, rrecv, xsend, xrecv, gsend, grecv,
    s1send, s1recv, s2send, s2recv,
):
    bi = lax.axis_index("batch")
    si = lax.axis_index("space")
    has_prev, has_next = si > 0, si < ns - 1
    prev, nxt = (bi, jnp.maximum(si - 1, 0)), (bi, jnp.minimum(si + 1, ns - 1))

    def space_peer(d):
        return (bi, lax.rem(si + d, ns))

    def batch_peer(d):
        return (lax.rem(bi + d, nb), si)

    barrier = pltpu.get_barrier_semaphore()

    def hello_space(d, carry):
        pl.semaphore_signal(barrier, inc=1, device_id=space_peer(d), device_id_type=MESH)
        return carry

    def hello_batch(d, carry):
        pl.semaphore_signal(barrier, inc=1, device_id=batch_peer(d), device_id_type=MESH)
        return carry

    lax.fori_loop(1, ns, hello_space, 0)
    lax.fori_loop(1, nb, hello_batch, 0)
    loads = [pltpu.make_async_copy(dens.at[:, :, z], buf.at[z], load_sem.at[z]) for z in range(2)]
    pairs = ((w1_hbm, w1), (fold_hbm, fold), (w2_hbm, w2), (b1_hbm, b1), (b2_hbm, b2), (cot_hbm, cot))
    params = [pltpu.make_async_copy(src, dst, in_sem.at[n]) for n, (src, dst) in enumerate(pairs)]
    for copy in loads + params:
        copy.start()
    pl.semaphore_wait(barrier, ns - 1 + nb - 1)

    def remote(src, dst, send, recv, target):
        return pltpu.make_async_remote_copy(
            src_ref=src, dst_ref=dst, send_sem=send, recv_sem=recv, device_id=target, device_id_type=MESH
        )

    dens_copies = [
        remote(dens.at[:, :, 1], buf.at[2], dsend.at[0], drecv.at[0], nxt),
        remote(dens.at[:, :, 0], buf.at[3], dsend.at[1], drecv.at[1], prev),
    ]
    pool_copies = [
        [
            remote(pooled.at[b], halo2.at[b, side], psend.at[b, side], precv.at[b, side], (nxt, prev)[side])
            for side in range(2)
        ]
        for b in range(2)
    ]
    back_copies = [
        [
            remote(bsend.at[b, side], brecv.at[b, side], ksend.at[b, side], krecv.at[b, side], (nxt, prev)[side])
            for side in range(2)
        ]
        for b in range(2)
    ]
    gives, takes = (has_next, has_prev), (has_prev, has_next)

    def start(copies):
        for side in range(2):
            pl.when(gives[side])(copies[side].start)

    def wait_in(copies):
        for side in range(2):
            pl.when(takes[side])(copies[side].wait_recv)

    def wait_out(copies):
        for side in range(2):
            pl.when(gives[side])(copies[side].wait_send)

    start(dens_copies)

    for side in range(2):
        def clear(side=side):
            buf[2 + side] = jnp.zeros(buf.shape[1:], BF16)
            for b in range(2):
                halo2[b, side] = jnp.zeros(halo2.shape[2:], BF16)
                brecv[b, side] = jnp.zeros(brecv.shape[2:], BF16)
        pl.when(jnp.logical_not(takes[side]))(clear)

    for copy in params:
        copy.wait()
    w1s[...] = jnp.zeros(w1s.shape, F32)
    w1s[:, 0:108] = w1[...].astype(F32)
    w1v = w1s[...].astype(BF16)
    for pos in range(8):
        wbig[pos * 32:(pos + 1) * 32, :] = dot(w1v, fold[:, pos * 256:(pos + 1) * 256]).astype(BF16)
    w2s[...] = jnp.zeros(w2s.shape, F32)
    w2s[:, 0:864] = w2[...].astype(F32)
    planes = (1, 0, 2)
    for j in range(3):
        for slot, i in enumerate(planes):
            lane = i * 288 + j * 96
            w2c[j * 64:(j + 1) * 64, slot * 96:(slot + 1) * 96] = w2s[:, lane:lane + 96].astype(BF16)
    for t4 in range(7):
        turned = w2s[:, t4 * 128:(t4 + 1) * 128].T
        for quarter in range(4):
            t = t4 * 4 + quarter
            if t < 27:
                i, j, k = t // 9, (t // 3) % 3, t % 3
                block = turned[quarter * 32:(quarter + 1) * 32, :]
                wb[j * 96 + i * 32:j * 96 + (i + 1) * 32, k * 64:(k + 1) * 64] = block.astype(BF16)
    bias1 = column_of(b1[...])
    bias1 = jnp.concatenate([bias1] * 8, axis=0)
    bias2 = column_of(b2[...])
    c9[...] = jnp.zeros(c9.shape, BF16)
    cb[...] = jnp.zeros(cb.shape, BF16)
    part[448:512, :] = jnp.zeros((64, 128), BF16)

    r, s = iota((256, 256), 0), iota((256, 256), 1)
    rows = (r & 192) + (r & 3) * 16 + ((r >> 3) & 7) * 2 + ((r >> 2) & 1)
    move_rows = (rows == s).astype(F32).astype(BF16)
    move_lanes = (r == (s & 127) * 2 + (s >> 7)).astype(F32).astype(BF16)

    def lay_out(pair):
        flat = buf[pair * 2:pair * 2 + 2].reshape(256, 256)
        moved = dot(move_rows, dot(flat, move_lanes).astype(BF16)).reshape(4, 8, 8, 256)
        gap = jnp.zeros((4, 1, 8, 256), F32)
        low = jnp.concatenate([gap, moved[:, :7]], axis=1)
        high = jnp.concatenate([moved[:, 1:], gap], axis=1)
        odd = iota(moved.shape, 2) >= 4
        beside = jnp.where(odd, low, high)
        for xg, field in enumerate((moved, beside)):
            even_y, odd_y = field[..., :128], field[..., 128:]
            for yg in range(2):
                halves = (even_y, odd_y) if yg == 0 else (after(even_y), before(odd_y))
                tile = jnp.concatenate(halves, axis=2).astype(BF16)
                for z in range(2):
                    row = ((pair * 2 + z) * 4 + xg * 2 + yg) * 16
                    for b in range(2):
                        for x in range(8):
                            lane = (b * 8 + x) * 128
                            cols1[row:row + 16, lane:lane + 128] = tile[z * 2 + b, x]

    for copy in loads:
        copy.wait()
    lay_out(0)
    wait_in(dens_copies)
    lay_out(1)

    def fill(target, row, height, b, field, flip):
        for x in range(8):
            lane = (b * 10 + 1 + x) * 128
            tile = field[:, x * 128:(x + 1) * 128]
            shifts = (before(tile), tile, after(tile))
            for k in range(3):
                piece = shifts[2 - k] if flip else shifts[k]
                target[row + k * height:row + (k + 1) * height, lane:lane + 128] = piece.astype(BF16)

    for b in range(2):
        for q in range(4):
            lane = b * 1024 + q * 256
            pre = dot(wbig[...], cols1[:, lane:lane + 256]) + bias1
            sig = sigmoid(pre)
            act = pre * sig
            d1[:, lane:lane + 256] = sig + act - act * sig
            total = act[0:32]
            for pos in range(1, 8):
                total = total + act[pos * 32:(pos + 1) * 32]
            pooled[b, :, q * 256:(q + 1) * 256] = (total * 0.125).astype(BF16)
        start(pool_copies[b])
    for b in range(2):
        fill(c9, 0, 32, b, pooled[b].astype(F32), False)
        acc2[b] = dot(w2c[:, 0:96], c9[0:96, b * 1280:(b + 1) * 1280])
        trans[b] = cot[b].astype(F32)

    gb2 = jnp.zeros((64, 1), F32)
    for b in range(2):
        wait_in(pool_copies[b])
        for side in range(2):
            fill(c9, 96 + side * 96, 32, b, halo2[b, side].astype(F32), False)
        acc = acc2[b] + dot(w2c[:, 96:288], c9[96:288, b * 1280:(b + 1) * 1280])
        pre = acc[0:64, 0:1024] + acc[64:128, 128:1152] + acc[128:192, 256:1280] + bias2
        sig = sigmoid(pre)
        act = pre * sig
        slope = sig + act - act * sig
        grads = []
        for x in range(8):
            grads.append(trans[b, pl.ds(x, 64, stride=8), :] * slope[:, x * 128:(x + 1) * 128])
        grad = jnp.concatenate(grads, axis=1).astype(BF16)
        gs[:, b * 1024:(b + 1) * 1024] = grad
        grad = grad.astype(F32)
        gb2 = gb2 + jnp.sum(grad, axis=1, keepdims=True)
        fill(cb, 0, 64, b, grad, True)
        acc = dot(wb[...], cb[:, b * 1280:(b + 1) * 1280])
        give = acc[0:96, 256:1280] + acc[96:192, 128:1152] + acc[192:288, 0:1024]
        bsend[b, 1] = give[0:32].astype(BF16)
        bsend[b, 0] = give[64:96].astype(BF16)
        start(back_copies[b])
        bown[:, b * 1024:(b + 1) * 1024] = give[32:64]
        for x in range(8):
            trans[b, pl.ds(x, 64, stride=8), :] = act[:, x * 128:(x + 1) * 128]
        feat[b] = trans[b].astype(BF16)

    for j in range(3):
        total = None
        for b in range(2):
            lane = b * 1280 + j * 128
            term = dot_nt(gs[:, b * 1024:(b + 1) * 1024], c9[:, lane:lane + 1024])
            total = term if total is None else total + term
        for slot, i in enumerate(planes):
            lane = i * 288 + j * 96
            w2s[:, lane:lane + 96] = total[:, slot * 96:(slot + 1) * 96]
    for t in range(7):
        part[t * 64:(t + 1) * 64, :] = w2s[:, t * 128:(t + 1) * 128].astype(BF16)

    size = 512 // ns

    def chunk(index):
        return pl.ds(pl.multiple_of(index * size, size), size)

    def rs_copy(d):
        return remote(part.at[chunk(lax.rem(si + d, ns))], rs_recv.at[d], rsend.at[d], rrecv.at[d], space_peer(d))

    def bx_copy(d):
        return remote(mine.at[0], bx_recv.at[bi], xsend.at[d], xrecv.at[d], batch_peer(d))

    def ag_copy(d):
        return remote(mine.at[1], full.at[chunk(si)], gsend.at[d], grecv.at[d], space_peer(d))

    def s1_copy(d):
        return remote(small, sm_recv.at[si], s1send.at[d], s1recv.at[d], space_peer(d))

    def s2_copy(d):
        return remote(sm_mid, sm_recv2.at[bi], s2send.at[d], s2recv.at[d], batch_peer(d))

    def each(count, make, act):
        def step(d, carry):
            act(make(d))
            return carry
        lax.fori_loop(1, count, step, 0)

    def go(copy):
        copy.start()

    def arrive(copy):
        copy.wait_recv()

    def leave(copy):
        copy.wait_send()

    def in_order(terms, count):
        total = terms[0].astype(F32)
        for index in range(1, count):
            total = total + terms[index].astype(F32)
        return total

    each(ns, rs_copy, go)

    gb1 = jnp.zeros((32, 256), F32)
    for b in range(2):
        wait_in(back_copies[b])
        for q in range(4):
            lane = b * 1024 + q * 256
            near = brecv[b, :, :, q * 256:(q + 1) * 256].astype(F32)
            back = (bown[:, lane:lane + 256] + near[0] + near[1]) * 0.125
            for pos in range(8):
                piece = (back * d1[pos * 32:(pos + 1) * 32, lane:lane + 256]).astype(BF16)
                gf[pos * 32:(pos + 1) * 32, lane:lane + 256] = piece
                gb1 = gb1 + piece.astype(F32)
    gram = dot_nt(gf[...], cols1[...])
    high = gram.astype(BF16)
    low = (gram - high.astype(F32)).astype(BF16)
    folded = jnp.zeros((64, 128), F32)
    for pos in range(8):
        both = jnp.concatenate([high[pos * 32:(pos + 1) * 32], low[pos * 32:(pos + 1) * 32]], axis=0)
        folded = folded + dot_nt(both, fold[:, pos * 256:(pos + 1) * 256])
    lane = iota((32, 128), 1)
    sums = folded[0:32] + folded[32:64]
    sums = jnp.where(lane == 108, jnp.sum(gb1, axis=1, keepdims=True), sums)
    sums = jnp.where(lane == 109, gb2[0:32], sums)
    small[...] = jnp.where(lane == 110, gb2[32:64], sums).astype(BF16)
    each(ns, s1_copy, go)

    each(ns, rs_copy, arrive)
    total = part[chunk(si), :].astype(F32)
    for d in range(1, ns):
        total = total + rs_recv[d].astype(F32)
    total = total.astype(BF16)
    mine[0] = total
    bx_recv[bi] = total
    each(nb, bx_copy, go)

    each(ns, s1_copy, arrive)
    sm_recv[si] = small[...]
    total = in_order(sm_recv, ns).astype(BF16)
    sm_mid[...] = total
    sm_recv2[bi] = total
    each(nb, s2_copy, go)

    each(nb, bx_copy, arrive)
    total = in_order(bx_recv, nb).astype(BF16)
    mine[1] = total
    full[chunk(si), :] = total
    each(ns, ag_copy, go)

    each(nb, s2_copy, arrive)
    total = in_order(sm_recv2, nb)
    gw1_out[...] = total[:, 0:108]
    gb1_out[...] = row_of(total[:, 108:109])
    gb2_out[...] = row_of(jnp.concatenate([total[:, 109:110], total[:, 110:111]], axis=0))

    each(ns, ag_copy, arrive)
    for t in range(7):
        width = min(128, 864 - t * 128)
        gw2_out[:, t * 128:t * 128 + width] = full[t * 64:(t + 1) * 64, 0:width].astype(F32)

    wait_out(dens_copies)
    for b in range(2):
        wait_out(pool_copies[b])
        wait_out(back_copies[b])
    each(ns, rs_copy, leave)
    each(nb, bx_copy, leave)
    each(ns, ag_copy, leave)
    each(ns, s1_copy, leave)
    each(nb, s2_copy, leave)


def hand_out(*refs):
    sources, results, held, sems = refs[0:5], refs[5:10], refs[10:15], refs[15]
    inward = [pltpu.make_async_copy(sources[n], held[n], sems.at[0, n]) for n in range(5)]
    outward = [pltpu.make_async_copy(held[n], results[n], sems.at[1, n]) for n in range(5)]
    for copy in inward:
        copy.start()
    for n in range(5):
        inward[n].wait()
        outward[n].start()
    for copy in outward:
        copy.wait()


def body(nb, ns, density, w_first, b_first, w_second, b_second, cotangent):
    vmem = pl.BlockSpec(memory_space=pltpu.VMEM)
    hbm = pl.BlockSpec(memory_space=pltpu.HBM)
    dma = pltpu.SemaphoreType.DMA
    size = 512 // ns
    shapes = (
        jax.ShapeDtypeStruct((2, 512, 128), BF16),
        jax.ShapeDtypeStruct((32, 108), F32),
        jax.ShapeDtypeStruct((1, 32), F32),
        jax.ShapeDtypeStruct((64, 864), F32),
        jax.ShapeDtypeStruct((1, 64), F32),
    )
    held = pl.pallas_call(
        functools.partial(kernel, nb, ns),
        out_shape=shapes,
        in_specs=[hbm] * 7,
        out_specs=(vmem,) * 5,
        scratch_shapes=[
            pltpu.VMEM((32, 108), BF16),
            pltpu.VMEM((1, 32), F32),
            pltpu.VMEM((64, 864), BF16),
            pltpu.VMEM((1, 64), F32),
            pltpu.VMEM((2, 512, 128), BF16),
            pltpu.VMEM((128, 2048), BF16),
            pltpu.VMEM((4, 2, 4, 16, 256), BF16),
            pltpu.VMEM((256, 2048), BF16),
            pltpu.VMEM((256, 256), BF16),
            pltpu.VMEM((256, 2048), F32),
            pltpu.VMEM((32, 128), F32),
            pltpu.VMEM((64, 896), F32),
            pltpu.VMEM((192, 288), BF16),
            pltpu.VMEM((288, 192), BF16),
            pltpu.VMEM((2, 32, 1024), BF16),
            pltpu.VMEM((2, 2, 32, 1024), BF16),
            pltpu.VMEM((288, 2560), BF16),
            pltpu.VMEM((2, 192, 1280), F32),
            pltpu.VMEM((2, 512, 128), F32),
            pltpu.VMEM((64, 2048), BF16),
            pltpu.VMEM((192, 2560), BF16),
            pltpu.VMEM((2, 2, 32, 1024), BF16),
            pltpu.VMEM((2, 2, 32, 1024), BF16),
            pltpu.VMEM((32, 2048), F32),
            pltpu.VMEM((256, 2048), BF16),
            pltpu.VMEM((512, 128), BF16),
            pltpu.VMEM((ns, size, 128), BF16),
            pltpu.VMEM((2, size, 128), BF16),
            pltpu.VMEM((nb, size, 128), BF16),
            pltpu.VMEM((512, 128), BF16),
            pltpu.VMEM((32, 128), BF16),
            pltpu.VMEM((ns, 32, 128), BF16),
            pltpu.VMEM((32, 128), BF16),
            pltpu.VMEM((nb, 32, 128), BF16),
            dma((2,)), dma((6,)), dma((2,)), dma((2,)),
            dma((2, 2)), dma((2, 2)), dma((2, 2)), dma((2, 2)),
            dma((ns,)), dma((ns,)), dma((nb,)), dma((nb,)), dma((ns,)), dma((ns,)),
            dma((ns,)), dma((ns,)), dma((nb,)), dma((nb,)),
        ],
        compiler_params=pltpu.CompilerParams(
            collective_id=0, has_side_effects=True, vmem_limit_bytes=62 * 1024 * 1024
        ),
        cost_estimate=pl.CostEstimate(flops=1 << 30, bytes_accessed=1 << 21, transcendentals=1 << 20),
    )(
        density, w_first, b_first.reshape(1, 32), w_second, b_second.reshape(1, 64), cotangent.reshape(2, 512, 128),
        jnp.asarray(fold_matrix(), BF16),
    )
    feat, gw1, gb1, gw2, gb2 = pl.pallas_call(
        hand_out,
        out_shape=shapes,
        in_specs=[hbm] * 5,
        out_specs=(hbm,) * 5,
        scratch_shapes=[pltpu.VMEM(one.shape, one.dtype) for one in shapes] + [dma((2, 5))],
        compiler_params=pltpu.CompilerParams(vmem_limit_bytes=62 * 1024 * 1024),
    )(*held)
    return feat.reshape(cotangent.shape), gw1, gb1.reshape(32), gw2, gb2.reshape(64)


def solution(mesh):
    data = P("batch", None, "space", None, None)
    return jax.shard_map(
        functools.partial(body, mesh.shape["batch"], mesh.shape["space"]),
        mesh=mesh,
        in_specs=(data, P(), P(), P(), P(), data),
        out_specs=(data, P(), P(), P(), P()),
        check_vma=False,
    )
```

profile of v0, /device:TPU:0, one launch (start us, length us, event | category | flops | bytes accessed | tf_op | source)
XLA Modules:
  0.0 32.3 jit_solution(15183798181733375636)
XLA Ops:
  0.6 29.9 %shard_map.110 = (bf16[2,512,128]{2,1,0:T(8,128)(2,1)}, f32[32,108]{1,0:T(8,128)}, f32[1,32]{1,0:T(1,128)}, f32[64,864]{1,0:T(8,128)}, f32[1,64]{1,0:T(1,128)}) custom-call(bf16[2,4,2,16,256]{4,3,2,1,0:T(8,128)(2,1)} %dens.1, bf16[32,108]{1,0:T(8,128)(2,1)} %w1_hbm.1, f32[1,32]{1,0:T(1,128)} %bitcast.10, bf16[64,864]{1,0:T(8,128)(2,1)} %w2_hbm.1, ...), custom_call_target="tpu_custom_call" | custom-call | flops 1073741824 | bytes 2097152 | tf_op jit(solution)/shard_map/pallas_call | solution.py:422
  30.5 1.8 %shard_map.111 = (bf16[2,512,128]{2,1,0:T(8,128)(2,1)}, f32[32,108]{1,0:T(8,128)}, f32[1,32]{1,0:T(1,128)}, f32[64,864]{1,0:T(8,128)}, f32[1,64]{1,0:T(1,128)}) custom-call(bf16[2,512,128]{2,1,0:T(8,128)(2,1)} %get-tuple-element.15.refs_0_, f32[32,108]{1,0:T(8,128)} %get-tuple-element.16.refs_1_, f32[1,32]{1,0:T(1,128)} %get-tuple-element.17.refs_2_, ...), custom_call_target="tpu_custom_call" | custom-call | tf_op jit(solution)/shard_map/pallas_call | solution.py:475
where the time goes:
time: 32.5 us; the launch traced here: 32.3 us
  Pallas kernels  31.7 us (98%)
  between operations  0.64 us (2%)
    pallas_call x1, Pallas kernels, body(): pl.pallas_call(functools.partial(kernel, nb, ns), out_shape=shapes, in_sp...  29.9 us
    pallas_call x1, Pallas kernels, body(): pl.pallas_call(hand_out, out_shape=shapes, in_specs=[hbm] * 5, out_specs=...  1.82 us

commit v1 on v0

--- a/solution.py
+++ b/solution.py
@@ -395,14 +395,10 @@
 
 
 def hand_out(*refs):
-    sources, results, held, sems = refs[0:5], refs[5:10], refs[10:15], refs[15]
-    inward = [pltpu.make_async_copy(sources[n], held[n], sems.at[0, n]) for n in range(5)]
-    outward = [pltpu.make_async_copy(held[n], results[n], sems.at[1, n]) for n in range(5)]
-    for copy in inward:
+    held, results, sems = refs[0:5], refs[5:10], refs[10]
+    outward = [pltpu.make_async_copy(held[n], results[n], sems.at[n]) for n in range(5)]
+    for copy in outward:
         copy.start()
-    for n in range(5):
-        inward[n].wait()
-        outward[n].start()
     for copy in outward:
         copy.wait()
 
@@ -421,7 +417,7 @@
     )
     held = pl.pallas_call(
         functools.partial(kernel, nb, ns),
-        out_shape=shapes,
+        out_shape=tuple(pltpu.VMEM(one.shape, one.dtype) for one in shapes),
         in_specs=[hbm] * 7,
         out_specs=(vmem,) * 5,
         scratch_shapes=[
@@ -465,20 +461,23 @@
             dma((ns,)), dma((ns,)), dma((nb,)), dma((nb,)),
         ],
         compiler_params=pltpu.CompilerParams(
-            collective_id=0, has_side_effects=True, vmem_limit_bytes=62 * 1024 * 1024
+            collective_id=0, has_side_effects=True, vmem_limit_bytes=40 * 1024 * 1024
         ),
         cost_estimate=pl.CostEstimate(flops=1 << 30, bytes_accessed=1 << 21, transcendentals=1 << 20),
-    )(
-        density, w_first, b_first.reshape(1, 32), w_second, b_second.reshape(1, 64), cotangent.reshape(2, 512, 128),
-        jnp.asarray(fold_matrix(), BF16),
-    )
+    )(*[
+        pltpu.with_memory_space_constraint(one, pltpu.HBM)
+        for one in (
+            density, w_first, b_first.reshape(1, 32), w_second, b_second.reshape(1, 64), cotangent.reshape(2, 512, 128),
+            jnp.asarray(fold_matrix(), BF16),
+        )
+    ])
     feat, gw1, gb1, gw2, gb2 = pl.pallas_call(
         hand_out,
         out_shape=shapes,
-        in_specs=[hbm] * 5,
+        in_specs=[vmem] * 5,
         out_specs=(hbm,) * 5,
-        scratch_shapes=[pltpu.VMEM(one.shape, one.dtype) for one in shapes] + [dma((2, 5))],
-        compiler_params=pltpu.CompilerParams(vmem_limit_bytes=62 * 1024 * 1024),
+        scratch_shapes=[dma((5,))],
+        compiler_params=pltpu.CompilerParams(vmem_limit_bytes=8 * 1024 * 1024),
     )(*held)
     return feat.reshape(cotangent.shape), gw1, gb1.reshape(32), gw2, gb2.reshape(64)
 

time: 32.5 us -> 30.7 us (0.945)
  Pallas kernels: 31.7 us -> 29.9 us
    pallas_call x2, Pallas kernels: 31.7 us -> 29.9 us  [the longest x1 29.1 us: body(): pl.pallas_call(functools.partial(kernel, nb, ns), out_shape=tuple((pltpu....]
where the time goes in v1:
time: 30.7 us; the launch traced here: 30.5 us
  Pallas kernels  29.9 us (97%)
  between operations  0.64 us (2%)
    pallas_call x1, Pallas kernels, body(): pl.pallas_call(functools.partial(kernel, nb, ns), out_shape=tuple((pltpu....  29.1 us
    pallas_call x1, Pallas kernels, body(): pl.pallas_call(hand_out, out_shape=shapes, in_specs=[vmem] * 5, out_specs...  0.83 us

profile of v1, /device:TPU:0, one launch (start us, length us, event | category | flops | bytes accessed | tf_op | source)
XLA Modules:
  0.0 30.5 jit_solution(12507263510758546702)
XLA Ops:
  0.6 29.1 %shard_map.110 = (bf16[2,512,128]{2,1,0:T(8,128)(2,1)S(1)}, f32[32,108]{1,0:T(8,128)S(1)}, f32[1,32]{1,0:T(1,128)S(1)}, f32[64,864]{1,0:T(8,128)S(1)}, f32[1,64]{1,0:T(1,128)S(1)}) custom-call(bf16[2,4,2,16,256]{4,3,2,1,0:T(8,128)(2,1)} %dens.1, bf16[32,108]{1,0:T(8,128)(2,1)} %w1_hbm.1, f32[1,32]{1,0:T(1,128)} %bitcast.10, bf16[64,864]{1,0:T(8,128)(2,1)} %w2_hbm.1, ...), custom_call_target="tpu_custom_call" | custom-call | flops 1073741824 | bytes 2097152 | tf_op jit(solution)/shard_map/pallas_call | solution.py:418
  29.7 0.8 %shard_map.111 = (bf16[2,512,128]{2,1,0:T(8,128)(2,1)}, f32[32,108]{1,0:T(8,128)}, f32[1,32]{1,0:T(1,128)}, f32[64,864]{1,0:T(8,128)}, f32[1,64]{1,0:T(1,128)}) custom-call(bf16[2,512,128]{2,1,0:T(8,128)(2,1)S(1)} %get-tuple-element.15.refs_0_, f32[32,108]{1,0:T(8,128)S(1)} %get-tuple-element.16.refs_1_, f32[1,32]{1,0:T(1,128)S(1)} %get-tuple-element.17.refs_2_, ...), custom_call_target="tpu_custom_call" | custom-call | tf_op jit(solution)/shard_map/pallas_call | solution.py:474

commit v2 on v1

--- a/solution.py
+++ b/solution.py
@@ -74,7 +74,7 @@
     nb, ns,
     dens, w1_hbm, b1_hbm, w2_hbm, b2_hbm, cot_hbm, fold_hbm,
     feat, gw1_out, gb1_out, gw2_out, gb2_out,
-    w1, b1, w2, b2, cot, fold, buf, cols1, wbig, d1, w1s, w2s, w2c, wb, pooled, halo2, c9, acc2, trans, gs, cb, bsend, brecv, bown, gf,
+    w1, b1, w2, b2, cot, fold, buf, cols1, wbig, d1, w1s, w2s, w2c, wb, pooled, halo2, c9, acc2, trans, acts, held, gs, cb, bsend, brecv, bown, gf,
     part, rs_recv, mine, bx_recv, full, small, sm_recv, sm_mid, sm_recv2,
     load_sem, in_sem, dsend, drecv, psend, precv, ksend, krecv, rsend, rrecv, xsend, xrecv, gsend, grecv,
     s1send, s1recv, s2send, s2recv,
@@ -92,21 +92,28 @@
 
     barrier = pltpu.get_barrier_semaphore()
 
-    def hello_space(d, carry):
-        pl.semaphore_signal(barrier, inc=1, device_id=space_peer(d), device_id_type=MESH)
-        return carry
-
-    def hello_batch(d, carry):
-        pl.semaphore_signal(barrier, inc=1, device_id=batch_peer(d), device_id_type=MESH)
-        return carry
-
-    lax.fori_loop(1, ns, hello_space, 0)
-    lax.fori_loop(1, nb, hello_batch, 0)
+    def hello(peer):
+        pl.semaphore_signal(barrier, inc=1, device_id=peer, device_id_type=MESH)
+
+    def every(numbers, act):
+        if len(numbers) <= 8:
+            for number in numbers:
+                act(number)
+        else:
+            def step(index, carry):
+                act(index + numbers[0])
+                return carry
+            lax.fori_loop(0, len(numbers), step, 0)
+
     loads = [pltpu.make_async_copy(dens.at[:, :, z], buf.at[z], load_sem.at[z]) for z in range(2)]
     pairs = ((w1_hbm, w1), (fold_hbm, fold), (w2_hbm, w2), (b1_hbm, b1), (b2_hbm, b2), (cot_hbm, cot))
     params = [pltpu.make_async_copy(src, dst, in_sem.at[n]) for n, (src, dst) in enumerate(pairs)]
     for copy in loads + params:
         copy.start()
+    hello(space_peer(1))
+    hello(space_peer(ns - 1))
+    every(range(2, ns - 1), lambda d: hello(space_peer(d)))
+    every(range(1, nb), lambda d: hello(batch_peer(d)))
     pl.semaphore_wait(barrier, ns - 1 + nb - 1)
 
     def remote(src, dst, send, recv, target):
@@ -115,8 +122,11 @@
         )
 
     dens_copies = [
-        remote(dens.at[:, :, 1], buf.at[2], dsend.at[0], drecv.at[0], nxt),
-        remote(dens.at[:, :, 0], buf.at[3], dsend.at[1], drecv.at[1], prev),
+        [
+            remote(buf.at[1 - side, b], buf.at[2 + side, b], dsend.at[b, side], drecv.at[b, side], (nxt, prev)[side])
+            for side in range(2)
+        ]
+        for b in range(2)
     ]
     pool_copies = [
         [
@@ -146,7 +156,10 @@
         for side in range(2):
             pl.when(gives[side])(copies[side].wait_send)
 
-    start(dens_copies)
+    for copy in loads:
+        copy.wait()
+    for b in range(2):
+        start(dens_copies[b])
 
     for side in range(2):
         def clear(side=side):
@@ -183,17 +196,18 @@
     bias2 = column_of(b2[...])
     c9[...] = jnp.zeros(c9.shape, BF16)
     cb[...] = jnp.zeros(cb.shape, BF16)
+    gs[...] = jnp.zeros(gs.shape, BF16)
     part[448:512, :] = jnp.zeros((64, 128), BF16)
 
     r, s = iota((256, 256), 0), iota((256, 256), 1)
     rows = (r & 192) + (r & 3) * 16 + ((r >> 3) & 7) * 2 + ((r >> 2) & 1)
-    move_rows = (rows == s).astype(F32).astype(BF16)
+    move_rows = (rows == s).astype(F32)[0:128, 0:128].astype(BF16)
     move_lanes = (r == (s & 127) * 2 + (s >> 7)).astype(F32).astype(BF16)
 
-    def lay_out(pair):
-        flat = buf[pair * 2:pair * 2 + 2].reshape(256, 256)
-        moved = dot(move_rows, dot(flat, move_lanes).astype(BF16)).reshape(4, 8, 8, 256)
-        gap = jnp.zeros((4, 1, 8, 256), F32)
+    def lay_out(pair, b):
+        flat = buf[pair * 2:pair * 2 + 2, b].reshape(128, 256)
+        moved = dot(move_rows, dot(flat, move_lanes).astype(BF16)).reshape(2, 8, 8, 256)
+        gap = jnp.zeros((2, 1, 8, 256), F32)
         low = jnp.concatenate([gap, moved[:, :7]], axis=1)
         high = jnp.concatenate([moved[:, 1:], gap], axis=1)
         odd = iota(moved.shape, 2) >= 4
@@ -205,16 +219,12 @@
                 tile = jnp.concatenate(halves, axis=2).astype(BF16)
                 for z in range(2):
                     row = ((pair * 2 + z) * 4 + xg * 2 + yg) * 16
-                    for b in range(2):
-                        for x in range(8):
-                            lane = (b * 8 + x) * 128
-                            cols1[row:row + 16, lane:lane + 128] = tile[z * 2 + b, x]
-
-    for copy in loads:
-        copy.wait()
-    lay_out(0)
-    wait_in(dens_copies)
-    lay_out(1)
+                    for x in range(8):
+                        lane = (b * 8 + x) * 128
+                        cols1[row:row + 16, lane:lane + 128] = tile[z, x]
+
+    for b in range(2):
+        lay_out(0, b)
 
     def fill(target, row, height, b, field, flip):
         for x in range(8):
@@ -226,6 +236,8 @@
                 target[row + k * height:row + (k + 1) * height, lane:lane + 128] = piece.astype(BF16)
 
     for b in range(2):
+        wait_in(dens_copies[b])
+        lay_out(1, b)
         for q in range(4):
             lane = b * 1024 + q * 256
             pre = dot(wbig[...], cols1[:, lane:lane + 256]) + bias1
@@ -242,7 +254,6 @@
         acc2[b] = dot(w2c[:, 0:96], c9[0:96, b * 1280:(b + 1) * 1280])
         trans[b] = cot[b].astype(F32)
 
-    gb2 = jnp.zeros((64, 1), F32)
     for b in range(2):
         wait_in(pool_copies[b])
         for side in range(2):
@@ -256,9 +267,10 @@
         for x in range(8):
             grads.append(trans[b, pl.ds(x, 64, stride=8), :] * slope[:, x * 128:(x + 1) * 128])
         grad = jnp.concatenate(grads, axis=1).astype(BF16)
-        gs[:, b * 1024:(b + 1) * 1024] = grad
+        for j in range(3):
+            lane = b * 1280 + j * 128
+            gs[j * 64:(j + 1) * 64, lane:lane + 1024] = grad
         grad = grad.astype(F32)
-        gb2 = gb2 + jnp.sum(grad, axis=1, keepdims=True)
         fill(cb, 0, 64, b, grad, True)
         acc = dot(wb[...], cb[:, b * 1280:(b + 1) * 1280])
         give = acc[0:96, 256:1280] + acc[96:192, 128:1152] + acc[192:288, 0:1024]
@@ -266,19 +278,13 @@
         bsend[b, 0] = give[64:96].astype(BF16)
         start(back_copies[b])
         bown[:, b * 1024:(b + 1) * 1024] = give[32:64]
-        for x in range(8):
-            trans[b, pl.ds(x, 64, stride=8), :] = act[:, x * 128:(x + 1) * 128]
-        feat[b] = trans[b].astype(BF16)
-
+        acts[b] = act
+
+    total = dot_nt(gs[...], c9[...])
     for j in range(3):
-        total = None
-        for b in range(2):
-            lane = b * 1280 + j * 128
-            term = dot_nt(gs[:, b * 1024:(b + 1) * 1024], c9[:, lane:lane + 1024])
-            total = term if total is None else total + term
         for slot, i in enumerate(planes):
             lane = i * 288 + j * 96
-            w2s[:, lane:lane + 96] = total[:, slot * 96:(slot + 1) * 96]
+            w2s[:, lane:lane + 96] = total[j * 64:(j + 1) * 64, slot * 96:(slot + 1) * 96]
     for t in range(7):
         part[t * 64:(t + 1) * 64, :] = w2s[:, t * 128:(t + 1) * 128].astype(BF16)
 
@@ -303,10 +309,7 @@
         return remote(sm_mid, sm_recv2.at[bi], s2send.at[d], s2recv.at[d], batch_peer(d))
 
     def each(count, make, act):
-        def step(d, carry):
-            act(make(d))
-            return carry
-        lax.fori_loop(1, count, step, 0)
+        every(range(1, count), lambda d: act(make(d)))
 
     def go(copy):
         copy.start()
@@ -324,6 +327,12 @@
         return total
 
     each(ns, rs_copy, go)
+
+    gb2 = jnp.sum(gs[64:128, :].astype(F32), axis=1, keepdims=True)
+    for b in range(2):
+        for x in range(8):
+            trans[b, pl.ds(x, 64, stride=8), :] = acts[b, :, x * 128:(x + 1) * 128]
+        feat[b] = trans[b].astype(BF16)
 
     gb1 = jnp.zeros((32, 256), F32)
     for b in range(2):
@@ -336,7 +345,10 @@
                 piece = (back * d1[pos * 32:(pos + 1) * 32, lane:lane + 256]).astype(BF16)
                 gf[pos * 32:(pos + 1) * 32, lane:lane + 256] = piece
                 gb1 = gb1 + piece.astype(F32)
-    gram = dot_nt(gf[...], cols1[...])
+        term = dot_nt(gf[:, b * 1024:(b + 1) * 1024], cols1[:, b * 1024:(b + 1) * 1024])
+        if b == 0:
+            held[...] = term
+    gram = held[...] + term
     high = gram.astype(BF16)
     low = (gram - high.astype(F32)).astype(BF16)
     folded = jnp.zeros((64, 128), F32)
@@ -378,20 +390,20 @@
     gb1_out[...] = row_of(total[:, 108:109])
     gb2_out[...] = row_of(jnp.concatenate([total[:, 109:110], total[:, 110:111]], axis=0))
 
+    for b in range(2):
+        wait_out(dens_copies[b])
+        wait_out(pool_copies[b])
+        wait_out(back_copies[b])
+    each(ns, rs_copy, leave)
+    each(nb, bx_copy, leave)
+    each(ns, s1_copy, leave)
+    each(nb, s2_copy, leave)
     each(ns, ag_copy, arrive)
     for t in range(7):
         width = min(128, 864 - t * 128)
         gw2_out[:, t * 128:t * 128 + width] = full[t * 64:(t + 1) * 64, 0:width].astype(F32)
 
-    wait_out(dens_copies)
-    for b in range(2):
-        wait_out(pool_copies[b])
-        wait_out(back_copies[b])
-    each(ns, rs_copy, leave)
-    each(nb, bx_copy, leave)
     each(ns, ag_copy, leave)
-    each(ns, s1_copy, leave)
-    each(nb, s2_copy, leave)
 
 
 def hand_out(*refs):
@@ -440,7 +452,9 @@
             pltpu.VMEM((288, 2560), BF16),
             pltpu.VMEM((2, 192, 1280), F32),
             pltpu.VMEM((2, 512, 128), F32),
-            pltpu.VMEM((64, 2048), BF16),
+            pltpu.VMEM((2, 64, 1024), F32),
+            pltpu.VMEM((256, 256), F32),
+            pltpu.VMEM((192, 2560), BF16),
             pltpu.VMEM((192, 2560), BF16),
             pltpu.VMEM((2, 2, 32, 1024), BF16),
             pltpu.VMEM((2, 2, 32, 1024), BF16),
@@ -455,7 +469,7 @@
             pltpu.VMEM((ns, 32, 128), BF16),
             pltpu.VMEM((32, 128), BF16),
             pltpu.VMEM((nb, 32, 128), BF16),
-            dma((2,)), dma((6,)), dma((2,)), dma((2,)),
+            dma((2,)), dma((6,)), dma((2, 2)), dma((2, 2)),
             dma((2, 2)), dma((2, 2)), dma((2, 2)), dma((2, 2)),
             dma((ns,)), dma((ns,)), dma((nb,)), dma((nb,)), dma((ns,)), dma((ns,)),
             dma((ns,)), dma((ns,)), dma((nb,)), dma((nb,)),

time: 30.7 us -> 29 us (0.945)
  Pallas kernels: 29.9 us -> 28.2 us
    pallas_call x1, Pallas kernels: 29.1 us -> 27.3 us  [body(): pl.pallas_call(functools.partial(kernel, nb, ns), out_shape=tuple((pltpu....]
where the time goes in v2:
time: 29 us; the launch traced here: 28.8 us
  Pallas kernels  28.2 us (97%)
  between operations  0.64 us (2%)
    pallas_call x1, Pallas kernels, body(): pl.pallas_call(functools.partial(kernel, nb, ns), out_shape=tuple((pltpu....  27.3 us
    pallas_call x1, Pallas kernels, body(): pl.pallas_call(hand_out, out_shape=shapes, in_specs=[vmem] * 5, out_specs...  0.83 us

profile of v2, /device:TPU:0, one launch (start us, length us, event | category | flops | bytes accessed | tf_op | source)
XLA Modules:
  0.0 28.8 jit_solution(4841460550099672468)
XLA Ops:
  0.6 27.3 %shard_map.110 = (bf16[2,512,128]{2,1,0:T(8,128)(2,1)S(1)}, f32[32,108]{1,0:T(8,128)S(1)}, f32[1,32]{1,0:T(1,128)S(1)}, f32[64,864]{1,0:T(8,128)S(1)}, f32[1,64]{1,0:T(1,128)S(1)}) custom-call(bf16[2,4,2,16,256]{4,3,2,1,0:T(8,128)(2,1)} %dens.1, bf16[32,108]{1,0:T(8,128)(2,1)} %w1_hbm.1, f32[1,32]{1,0:T(1,128)} %bitcast.10, bf16[64,864]{1,0:T(8,128)(2,1)} %w2_hbm.1, ...), custom_call_target="tpu_custom_call" | custom-call | flops 1073741824 | bytes 2097152 | tf_op jit(solution)/shard_map/pallas_call | solution.py:430
  28.0 0.8 %shard_map.111 = (bf16[2,512,128]{2,1,0:T(8,128)(2,1)}, f32[32,108]{1,0:T(8,128)}, f32[1,32]{1,0:T(1,128)}, f32[64,864]{1,0:T(8,128)}, f32[1,64]{1,0:T(1,128)}) custom-call(bf16[2,512,128]{2,1,0:T(8,128)(2,1)S(1)} %get-tuple-element.15.refs_0_, f32[32,108]{1,0:T(8,128)S(1)} %get-tuple-element.16.refs_1_, f32[1,32]{1,0:T(1,128)S(1)} %get-tuple-element.17.refs_2_, ...), custom_call_target="tpu_custom_call" | custom-call | tf_op jit(solution)/shard_map/pallas_call | solution.py:488

commit v3 on v2

--- a/solution.py
+++ b/solution.py
@@ -326,7 +326,18 @@
             total = total + terms[index].astype(F32)
         return total
 
-    each(ns, rs_copy, go)
+    live = -(-448 // size)
+
+    def rs_go(d):
+        pl.when(lax.rem(si + d, ns) < live)(rs_copy(d).start)
+
+    def rs_leave(d):
+        pl.when(lax.rem(si + d, ns) < live)(rs_copy(d).wait_send)
+
+    def ag_arrive(d):
+        pl.when(lax.rem(si + ns - d, ns) < live)(ag_copy(d).wait_recv)
+
+    every(range(1, ns), rs_go)
 
     gb2 = jnp.sum(gs[64:128, :].astype(F32), axis=1, keepdims=True)
     for b in range(2):
@@ -362,14 +373,16 @@
     small[...] = jnp.where(lane == 110, gb2[32:64], sums).astype(BF16)
     each(ns, s1_copy, go)
 
-    each(ns, rs_copy, arrive)
-    total = part[chunk(si), :].astype(F32)
-    for d in range(1, ns):
-        total = total + rs_recv[d].astype(F32)
-    total = total.astype(BF16)
-    mine[0] = total
-    bx_recv[bi] = total
-    each(nb, bx_copy, go)
+    @pl.when(si < live)
+    def space_sum():
+        each(ns, rs_copy, arrive)
+        total = part[chunk(si), :].astype(F32)
+        for d in range(1, ns):
+            total = total + rs_recv[d].astype(F32)
+        total = total.astype(BF16)
+        mine[0] = total
+        bx_recv[bi] = total
+        each(nb, bx_copy, go)
 
     each(ns, s1_copy, arrive)
     sm_recv[si] = small[...]
@@ -378,11 +391,13 @@
     sm_recv2[bi] = total
     each(nb, s2_copy, go)
 
-    each(nb, bx_copy, arrive)
-    total = in_order(bx_recv, nb).astype(BF16)
-    mine[1] = total
-    full[chunk(si), :] = total
-    each(ns, ag_copy, go)
+    @pl.when(si < live)
+    def batch_sum():
+        each(nb, bx_copy, arrive)
+        total = in_order(bx_recv, nb).astype(BF16)
+        mine[1] = total
+        full[chunk(si), :] = total
+        each(ns, ag_copy, go)
 
     each(nb, s2_copy, arrive)
     total = in_order(sm_recv2, nb)
@@ -394,16 +409,18 @@
         wait_out(dens_copies[b])
         wait_out(pool_copies[b])
         wait_out(back_copies[b])
-    each(ns, rs_copy, leave)
-    each(nb, bx_copy, leave)
+    every(range(1, ns), rs_leave)
     each(ns, s1_copy, leave)
     each(nb, s2_copy, leave)
-    each(ns, ag_copy, arrive)
+    every(range(1, ns), ag_arrive)
     for t in range(7):
         width = min(128, 864 - t * 128)
         gw2_out[:, t * 128:t * 128 + width] = full[t * 64:(t + 1) * 64, 0:width].astype(F32)
 
-    each(ns, ag_copy, leave)
+    @pl.when(si < live)
+    def done():
+        each(nb, bx_copy, leave)
+        each(ns, ag_copy, leave)
 
 
 def hand_out(*refs):

time: 29 us -> 28.7 us (0.990)
  Pallas kernels: 28.2 us -> 27.9 us
where the time goes in v3:
time: 28.7 us; the launch traced here: 28.5 us
  Pallas kernels  27.9 us (97%)
  between operations  0.64 us (2%)
    pallas_call x1, Pallas kernels, body(): pl.pallas_call(functools.partial(kernel, nb, ns), out_shape=tuple((pltpu....  27.1 us
    pallas_call x1, Pallas kernels, body(): pl.pallas_call(hand_out, out_shape=shapes, in_specs=[vmem] * 5, out_specs...  0.83 us

profile of v3, /device:TPU:0, one launch (start us, length us, event | category | flops | bytes accessed | tf_op | source)
XLA Modules:
  0.0 28.5 jit_solution(129974690284059926)
XLA Ops:
  0.6 27.1 %shard_map.110 = (bf16[2,512,128]{2,1,0:T(8,128)(2,1)S(1)}, f32[32,108]{1,0:T(8,128)S(1)}, f32[1,32]{1,0:T(1,128)S(1)}, f32[64,864]{1,0:T(8,128)S(1)}, f32[1,64]{1,0:T(1,128)S(1)}) custom-call(bf16[2,4,2,16,256]{4,3,2,1,0:T(8,128)(2,1)} %dens.1, bf16[32,108]{1,0:T(8,128)(2,1)} %w1_hbm.1, f32[1,32]{1,0:T(1,128)} %bitcast.10, bf16[64,864]{1,0:T(8,128)(2,1)} %w2_hbm.1, ...), custom_call_target="tpu_custom_call" | custom-call | flops 1073741824 | bytes 2097152 | tf_op jit(solution)/shard_map/pallas_call | solution.py:447
  27.7 0.8 %shard_map.111 = (bf16[2,512,128]{2,1,0:T(8,128)(2,1)}, f32[32,108]{1,0:T(8,128)}, f32[1,32]{1,0:T(1,128)}, f32[64,864]{1,0:T(8,128)}, f32[1,64]{1,0:T(1,128)}) custom-call(bf16[2,512,128]{2,1,0:T(8,128)(2,1)S(1)} %get-tuple-element.15.refs_0_, f32[32,108]{1,0:T(8,128)S(1)} %get-tuple-element.16.refs_1_, f32[1,32]{1,0:T(1,128)S(1)} %get-tuple-element.17.refs_2_, ...), custom_call_target="tpu_custom_call" | custom-call | tf_op jit(solution)/shard_map/pallas_call | solution.py:505

commit v4 on v3

--- a/solution.py
+++ b/solution.py
@@ -130,10 +130,13 @@
     ]
     pool_copies = [
         [
-            remote(pooled.at[b], halo2.at[b, side], psend.at[b, side], precv.at[b, side], (nxt, prev)[side])
+            remote(
+                pooled.at[piece // 2, :, pl.ds(piece % 2 * 512, 512)], halo2.at[piece // 2, side, :, pl.ds(piece % 2 * 512, 512)],
+                psend.at[piece, side], precv.at[piece, side], (nxt, prev)[side],
+            )
             for side in range(2)
         ]
-        for b in range(2)
+        for piece in range(4)
     ]
     back_copies = [
         [
@@ -144,9 +147,12 @@
     ]
     gives, takes = (has_next, has_prev), (has_prev, has_next)
 
+    odd = lax.rem(si, 2) == 1
+
     def start(copies):
-        for side in range(2):
-            pl.when(gives[side])(copies[side].start)
+        for turn in (odd, jnp.logical_not(odd)):
+            pl.when(jnp.logical_and(gives[0], turn))(copies[0].start)
+            pl.when(jnp.logical_and(gives[1], jnp.logical_not(turn)))(copies[1].start)
 
     def wait_in(copies):
         for side in range(2):
@@ -248,14 +254,16 @@
             for pos in range(1, 8):
                 total = total + act[pos * 32:(pos + 1) * 32]
             pooled[b, :, q * 256:(q + 1) * 256] = (total * 0.125).astype(BF16)
-        start(pool_copies[b])
+            if q % 2 == 1:
+                start(pool_copies[b * 2 + q // 2])
     for b in range(2):
         fill(c9, 0, 32, b, pooled[b].astype(F32), False)
         acc2[b] = dot(w2c[:, 0:96], c9[0:96, b * 1280:(b + 1) * 1280])
         trans[b] = cot[b].astype(F32)
 
     for b in range(2):
-        wait_in(pool_copies[b])
+        wait_in(pool_copies[b * 2])
+        wait_in(pool_copies[b * 2 + 1])
         for side in range(2):
             fill(c9, 96 + side * 96, 32, b, halo2[b, side].astype(F32), False)
         acc = acc2[b] + dot(w2c[:, 96:288], c9[96:288, b * 1280:(b + 1) * 1280])
@@ -399,18 +407,19 @@
         full[chunk(si), :] = total
         each(ns, ag_copy, go)
 
+    for b in range(2):
+        wait_out(dens_copies[b])
+        wait_out(pool_copies[b * 2])
+        wait_out(pool_copies[b * 2 + 1])
+        wait_out(back_copies[b])
+    every(range(1, ns), rs_leave)
+    each(ns, s1_copy, leave)
     each(nb, s2_copy, arrive)
     total = in_order(sm_recv2, nb)
     gw1_out[...] = total[:, 0:108]
     gb1_out[...] = row_of(total[:, 108:109])
     gb2_out[...] = row_of(jnp.concatenate([total[:, 109:110], total[:, 110:111]], axis=0))
 
-    for b in range(2):
-        wait_out(dens_copies[b])
-        wait_out(pool_copies[b])
-        wait_out(back_copies[b])
-    every(range(1, ns), rs_leave)
-    each(ns, s1_copy, leave)
     each(nb, s2_copy, leave)
     every(range(1, ns), ag_arrive)
     for t in range(7):
@@ -487,7 +496,7 @@
             pltpu.VMEM((32, 128), BF16),
             pltpu.VMEM((nb, 32, 128), BF16),
             dma((2,)), dma((6,)), dma((2, 2)), dma((2, 2)),
-            dma((2, 2)), dma((2, 2)), dma((2, 2)), dma((2, 2)),
+            dma((4, 2)), dma((4, 2)), dma((2, 2)), dma((2, 2)),
             dma((ns,)), dma((ns,)), dma((nb,)), dma((nb,)), dma((ns,)), dma((ns,)),
             dma((ns,)), dma((ns,)), dma((nb,)), dma((nb,)),
         ],

time: 28.7 us -> 28.6 us (level)
  no operation moved by 1% of the time
where the time goes in v4:
time: 28.6 us; the launch traced here: 28.4 us
  Pallas kernels  27.8 us (97%)
  between operations  0.64 us (2%)
    pallas_call x1, Pallas kernels, body(): pl.pallas_call(functools.partial(kernel, nb, ns), out_shape=tuple((pltpu....  26.9 us
    pallas_call x1, Pallas kernels, body(): pl.pallas_call(hand_out, out_shape=shapes, in_specs=[vmem] * 5, out_specs...  0.83 us

profile of v4, /device:TPU:0, one launch (start us, length us, event | category | flops | bytes accessed | tf_op | source)
XLA Modules:
  0.0 28.4 jit_solution(3040804014608706189)
XLA Ops:
  0.6 26.9 %shard_map.110 = (bf16[2,512,128]{2,1,0:T(8,128)(2,1)S(1)}, f32[32,108]{1,0:T(8,128)S(1)}, f32[1,32]{1,0:T(1,128)S(1)}, f32[64,864]{1,0:T(8,128)S(1)}, f32[1,64]{1,0:T(1,128)S(1)}) custom-call(bf16[2,4,2,16,256]{4,3,2,1,0:T(8,128)(2,1)} %dens.1, bf16[32,108]{1,0:T(8,128)(2,1)} %w1_hbm.1, f32[1,32]{1,0:T(1,128)} %bitcast.10, bf16[64,864]{1,0:T(8,128)(2,1)} %w2_hbm.1, ...), custom_call_target="tpu_custom_call" | custom-call | flops 1073741824 | bytes 2097152 | tf_op jit(solution)/shard_map/pallas_call | solution.py:456
  27.6 0.8 %shard_map.111 = (bf16[2,512,128]{2,1,0:T(8,128)(2,1)}, f32[32,108]{1,0:T(8,128)}, f32[1,32]{1,0:T(1,128)}, f32[64,864]{1,0:T(8,128)}, f32[1,64]{1,0:T(1,128)}) custom-call(bf16[2,512,128]{2,1,0:T(8,128)(2,1)S(1)} %get-tuple-element.15.refs_0_, f32[32,108]{1,0:T(8,128)S(1)} %get-tuple-element.16.refs_1_, f32[1,32]{1,0:T(1,128)S(1)} %get-tuple-element.17.refs_2_, ...), custom_call_target="tpu_custom_call" | custom-call | tf_op jit(solution)/shard_map/pallas_call | solution.py:514

commit v5 on v4

--- a/solution.py
+++ b/solution.py
@@ -232,10 +232,10 @@
     for b in range(2):
         lay_out(0, b)
 
-    def fill(target, row, height, b, field, flip):
-        for x in range(8):
+    def fill(target, row, height, b, field, flip, cells=range(8)):
+        for x in cells:
             lane = (b * 10 + 1 + x) * 128
-            tile = field[:, x * 128:(x + 1) * 128]
+            tile = field[:, x * 128:(x + 1) * 128].astype(F32)
             shifts = (before(tile), tile, after(tile))
             for k in range(3):
                 piece = shifts[2 - k] if flip else shifts[k]
@@ -262,10 +262,10 @@
         trans[b] = cot[b].astype(F32)
 
     for b in range(2):
-        wait_in(pool_copies[b * 2])
-        wait_in(pool_copies[b * 2 + 1])
-        for side in range(2):
-            fill(c9, 96 + side * 96, 32, b, halo2[b, side].astype(F32), False)
+        for half in range(2):
+            wait_in(pool_copies[b * 2 + half])
+            for side in range(2):
+                fill(c9, 96 + side * 96, 32, b, halo2.at[b, side], False, range(half * 4, half * 4 + 4))
         acc = acc2[b] + dot(w2c[:, 96:288], c9[96:288, b * 1280:(b + 1) * 1280])
         pre = acc[0:64, 0:1024] + acc[64:128, 128:1152] + acc[128:192, 256:1280] + bias2
         sig = sigmoid(pre)

time: 28.6 us -> 28.5 us (level)
  no operation moved by 1% of the time
where the time goes in v5:
time: 28.5 us; the launch traced here: 28.4 us
  Pallas kernels  27.7 us (97%)
  between operations  0.64 us (2%)
    pallas_call x1, Pallas kernels, body(): pl.pallas_call(functools.partial(kernel, nb, ns), out_shape=tuple((pltpu....  26.9 us
    pallas_call x1, Pallas kernels, body(): pl.pallas_call(hand_out, out_shape=shapes, in_specs=[vmem] * 5, out_specs...  0.83 us

profile of v5, /device:TPU:0, one launch (start us, length us, event | category | flops | bytes accessed | tf_op | source)
XLA Modules:
  0.0 28.4 jit_solution(1094806707079156578)
XLA Ops:
  0.6 26.9 %shard_map.110 = (bf16[2,512,128]{2,1,0:T(8,128)(2,1)S(1)}, f32[32,108]{1,0:T(8,128)S(1)}, f32[1,32]{1,0:T(1,128)S(1)}, f32[64,864]{1,0:T(8,128)S(1)}, f32[1,64]{1,0:T(1,128)S(1)}) custom-call(bf16[2,4,2,16,256]{4,3,2,1,0:T(8,128)(2,1)} %dens.1, bf16[32,108]{1,0:T(8,128)(2,1)} %w1_hbm.1, f32[1,32]{1,0:T(1,128)} %bitcast.10, bf16[64,864]{1,0:T(8,128)(2,1)} %w2_hbm.1, ...), custom_call_target="tpu_custom_call" | custom-call | flops 1073741824 | bytes 2097152 | tf_op jit(solution)/shard_map/pallas_call | solution.py:456
  27.6 0.8 %shard_map.111 = (bf16[2,512,128]{2,1,0:T(8,128)(2,1)}, f32[32,108]{1,0:T(8,128)}, f32[1,32]{1,0:T(1,128)}, f32[64,864]{1,0:T(8,128)}, f32[1,64]{1,0:T(1,128)}) custom-call(bf16[2,512,128]{2,1,0:T(8,128)(2,1)S(1)} %get-tuple-element.15.refs_0_, f32[32,108]{1,0:T(8,128)S(1)} %get-tuple-element.16.refs_1_, f32[1,32]{1,0:T(1,128)S(1)} %get-tuple-element.17.refs_2_, ...), custom_call_target="tpu_custom_call" | custom-call | tf_op jit(solution)/shard_map/pallas_call | solution.py:514

commit v6 on v5

--- a/solution.py
+++ b/solution.py
@@ -370,10 +370,10 @@
     gram = held[...] + term
     high = gram.astype(BF16)
     low = (gram - high.astype(F32)).astype(BF16)
-    folded = jnp.zeros((64, 128), F32)
-    for pos in range(8):
-        both = jnp.concatenate([high[pos * 32:(pos + 1) * 32], low[pos * 32:(pos + 1) * 32]], axis=0)
-        folded = folded + dot_nt(both, fold[:, pos * 256:(pos + 1) * 256])
+    both = jnp.concatenate([
+        jnp.concatenate([term[pos * 32:(pos + 1) * 32] for pos in range(8)], axis=1) for term in (high, low)
+    ], axis=0)
+    folded = dot_nt(both, fold[...])
     lane = iota((32, 128), 1)
     sums = folded[0:32] + folded[32:64]
     sums = jnp.where(lane == 108, jnp.sum(gb1, axis=1, keepdims=True), sums)

time: 28.5 us -> 28.5 us (level)
  no operation moved by 1% of the time
where the time goes in v6:
time: 28.5 us; the launch traced here: 28.4 us
  Pallas kernels  27.7 us (97%)
  between operations  0.64 us (2%)
    pallas_call x1, Pallas kernels, body(): pl.pallas_call(functools.partial(kernel, nb, ns), out_shape=tuple((pltpu....  26.9 us
    pallas_call x1, Pallas kernels, body(): pl.pallas_call(hand_out, out_shape=shapes, in_specs=[vmem] * 5, out_specs...  0.83 us

profile of v6, /device:TPU:0, one launch (start us, length us, event | category | flops | bytes accessed | tf_op | source)
XLA Modules:
  0.0 28.4 jit_solution(9841743101848139647)
XLA Ops:
  0.6 26.9 %shard_map.110 = (bf16[2,512,128]{2,1,0:T(8,128)(2,1)S(1)}, f32[32,108]{1,0:T(8,128)S(1)}, f32[1,32]{1,0:T(1,128)S(1)}, f32[64,864]{1,0:T(8,128)S(1)}, f32[1,64]{1,0:T(1,128)S(1)}) custom-call(bf16[2,4,2,16,256]{4,3,2,1,0:T(8,128)(2,1)} %dens.1, bf16[32,108]{1,0:T(8,128)(2,1)} %w1_hbm.1, f32[1,32]{1,0:T(1,128)} %bitcast.10, bf16[64,864]{1,0:T(8,128)(2,1)} %w2_hbm.1, ...), custom_call_target="tpu_custom_call" | custom-call | flops 1073741824 | bytes 2097152 | tf_op jit(solution)/shard_map/pallas_call | solution.py:456
  27.6 0.8 %shard_map.111 = (bf16[2,512,128]{2,1,0:T(8,128)(2,1)}, f32[32,108]{1,0:T(8,128)}, f32[1,32]{1,0:T(1,128)}, f32[64,864]{1,0:T(8,128)}, f32[1,64]{1,0:T(1,128)}) custom-call(bf16[2,512,128]{2,1,0:T(8,128)(2,1)S(1)} %get-tuple-element.15.refs_0_, f32[32,108]{1,0:T(8,128)S(1)} %get-tuple-element.16.refs_1_, f32[1,32]{1,0:T(1,128)S(1)} %get-tuple-element.17.refs_2_, ...), custom_call_target="tpu_custom_call" | custom-call | tf_op jit(solution)/shard_map/pallas_call | solution.py:514
